TPU v7x, 256 devices: a whole 4x4x8 slice. The times are simulated.
256 devices in a mesh: table: 64 (over y, z, core), col: 4 (over x).
Axes of the slice: x: 4, y: 4, z: 8, core: 2. Of those that a mesh axis runs over, the one named last changes fastest.
Arguments:
- embedding: bfloat16 [262144, 256], P('table', 'col'), may hold values from -4 to 4
- accumulator: float32 [262144, 256], P('table', 'col'), may hold values from 0.01 to 1
- pair_rows: int32 [16384, 128, 4], P(('table', 'col')), may hold values from 0 to 1023
- pair_len: int32 [16384, 128], P(('table', 'col')), may hold values from 0 to 4
- pair_dest: int32 [256, 64], P(('table', 'col')), may hold values from 0 to 63, each once within a row
- pair_tile: int32 [256, 64], P(('table', 'col')), may hold values from 0 to 15
- pooled_grad: bfloat16 [524288, 256], P(('table', 'col')), may hold values from -6 to 6
Outputs:
- pooled: bfloat16 [524288, 256], P(('table', 'col'))
- new_embedding: bfloat16 [262144, 256], P(('table', 'col'))
- new_accumulator: float32 [262144, 256], P(('table', 'col'))
Inputs may be any that keep to these rules, and one draw needn't show every extreme that they name: `pair_dest`: each row names every table index exactly once.
All inputs are finite; a program needn't handle non-finite values.
Results may differ from a plain program's by a relative error of at most 0.0049.
Values may be sent and summed in bfloat16 or wider, within the bound.
A program may use at most 128 MiB of HBM per device.

v0:
```python
import jax
import jax.numpy as jnp
from jax import lax
from jax.sharding import PartitionSpec as P

LEARN_RATE = 0.3
EPSILON = 1e-08


def incidence(rows, lengths, width):
    valid = jnp.arange(rows.shape[-1], dtype=jnp.int32)[None, None, :] < lengths[:, :, None]
    hits = (rows[..., None] == jnp.arange(width, dtype=jnp.int32)) & valid[..., None]
    return jnp.sum(hits.astype(jnp.bfloat16), axis=2)


def move_state(accumulator):
    return lax.all_to_all(
        accumulator.astype(jnp.bfloat16), "col", split_axis=0, concat_axis=1, tiled=True
    ).astype(accumulator.dtype)


def per_device(embedding, accumulator, pair_rows, pair_len, pair_dest, pair_tile, pooled_grad):
    table_count = lax.axis_size("table")
    pair_count = pair_rows.shape[0]
    bag_rows = pair_rows.shape[1]
    width = embedding.shape[1] * lax.axis_size("col")
    tile_count = pooled_grad.shape[0] // bag_rows
    span = min(8, pair_count)
    groups = pair_count // span
    owned = lax.all_to_all(embedding, "col", split_axis=0, concat_axis=1, tiled=True)
    state = move_state(accumulator)
    row_count = owned.shape[0]
    rows_grouped = pair_rows.reshape(groups, span, bag_rows, pair_rows.shape[2])
    lens_grouped = pair_len.reshape(groups, span, bag_rows)
    dest_onehot = (
        pair_dest[0][None, :] == jnp.arange(table_count, dtype=jnp.int32)[:, None]
    ).astype(jnp.bfloat16)
    tile_marks = (pair_tile[0] + 1).astype(jnp.bfloat16)[:, None]
    send_tiles = jnp.dot(dest_onehot, tile_marks, preferred_element_type=jnp.float32).astype(
        jnp.bfloat16
    )
    tile_numbers = jnp.arange(tile_count, dtype=jnp.float32) + 1.0
    grad_tiles = pooled_grad.reshape(tile_count, bag_rows, width)

    def pool_group(item):
        rows, lengths = item
        counts = incidence(rows, lengths, row_count)
        part = jnp.einsum("gbr,rd->gbd", counts, owned, preferred_element_type=jnp.float32)
        return (part.astype(jnp.bfloat16), counts)

    partial_value, saved_counts = lax.map(pool_group, (rows_grouped, lens_grouped))
    partial_value = partial_value.reshape(pair_count, bag_rows, width)
    send_blocks = jnp.einsum(
        "np,pbd->nbd", dest_onehot, partial_value, preferred_element_type=jnp.float32
    ).astype(jnp.bfloat16)
    arrived, arrived_tiles = (
        lax.all_to_all(send_blocks, "table", split_axis=0, concat_axis=0, tiled=True),
        lax.all_to_all(send_tiles, "table", split_axis=0, concat_axis=0, tiled=True),
    )
    tile_onehot = (
        arrived_tiles[:, 0].astype(jnp.float32)[None, :] == tile_numbers[:, None]
    ).astype(jnp.bfloat16)
    back_blocks = jnp.einsum(
        "tn,tbd->nbd", tile_onehot, grad_tiles, preferred_element_type=jnp.float32
    ).astype(jnp.bfloat16)
    pooled = jnp.einsum("tn,nbd->tbd", tile_onehot, arrived, preferred_element_type=jnp.float32)
    pooled = pooled.astype(jnp.bfloat16).reshape(tile_count * bag_rows, width)
    returned = lax.all_to_all(back_blocks, "table", split_axis=0, concat_axis=0, tiled=True)
    pair_grads = jnp.einsum(
        "np,nbd->pbd", dest_onehot, returned, preferred_element_type=jnp.float32
    ).astype(jnp.bfloat16)
    pair_grads = pair_grads.reshape(groups, span, bag_rows, width)

    def add_group(total, item):
        counts, grads = item
        return (
            total + jnp.einsum("gbr,gbd->rd", counts, grads, preferred_element_type=jnp.float32),
            None,
        )

    empty = jnp.zeros((row_count, width), jnp.float32)
    grad, unused = lax.scan(add_group, empty, (saved_counts, pair_grads))
    new_state = state + grad * grad
    new_rows = (
        owned.astype(jnp.float32) - LEARN_RATE * grad / (jnp.sqrt(new_state) + EPSILON)
    ).astype(jnp.bfloat16)
    return (pooled, new_rows, new_state)


def solution(mesh):
    return jax.shard_map(
        per_device,
        mesh=mesh,
        in_specs=(
            P("table", "col"),
            P("table", "col"),
            P(("table", "col"), None, None),
            P(("table", "col"), None),
            P(("table", "col"), None),
            P(("table", "col"), None),
            P(("table", "col"), None),
        ),
        out_specs=(P(("table", "col"), None), P(("table", "col"), None), P(("table", "col"), None)),
        check_vma=False,
    )
```

profile of v0, /device:TPU:1, one launch (start us, length us, event | category | flops | bytes accessed | tf_op | source)
XLA Modules:
  0.0 259.6 jit_solution(2965978162360990122)
XLA Ops:
  2.3 13.2 %all-to-all-start = ((bf16[64,1,1]{2,1,0:T(2,128)(2,1)}), bf16[64,1,1]{2,1,0:T(2,128)(2,1)S(1)}, u32[]{:S(2)}, u32[]{:S(2)}) async-start(bf16[64,1,1]{2,1,0:T(2,128)(2,1)} %copy.86), calls=%async_computation | async-start | bytes 65536 | tf_op jit(solution)/shard_map/all_to_all | solution.py:58
  15.5 1.9 copy.137
  17.4 7.3 %all-to-all-done = bf16[64,1,1]{2,1,0:T(2,128)(2,1)S(1)} async-done(((bf16[64,1,1]{2,1,0:T(2,128)(2,1)}), bf16[64,1,1]{2,1,0:T(2,128)(2,1)S(1)}, u32[]{:S(2)}, u32[]{:S(2)}) %all-to-all-start) | async-done | bytes 160 | tf_op jit(solution)/shard_map/all_to_all | solution.py:58
  24.7 4.0 %all-to-all-start.1 = ((bf16[4,1024,64]{1,2,0:T(8,128)(2,1)}), bf16[4,1024,64]{1,2,0:T(8,128)(2,1)S(1)}, u32[]{:S(2)}, u32[]{:S(2)}) async-start(bf16[4,1024,64]{1,2,0:T(8,128)(2,1)} %bitcast.77), calls=%async_computation.1 | async-start | bytes 1048576 | tf_op jit(solution)/shard_map/all_to_all | solution.py:30
  28.7 1.3 convert_element_type.78
  30.8 6.2 %all-to-all-done.1 = bf16[4,1024,64]{1,2,0:T(8,128)(2,1)S(1)} async-done(((bf16[4,1024,64]{1,2,0:T(8,128)(2,1)}), bf16[4,1024,64]{1,2,0:T(8,128)(2,1)S(1)}, u32[]{:S(2)}, u32[]{:S(2)}) %all-to-all-start.1) | async-done | bytes 524320 | tf_op jit(solution)/shard_map/all_to_all | solution.py:30
  37.0 3.5 %all-to-all-start.4 = ((bf16[4,1024,64]{1,2,0:T(8,128)(2,1)}), bf16[4,1024,64]{1,2,0:T(8,128)(2,1)S(1)}, u32[]{:S(2)}, u32[]{:S(2)}) async-start(bf16[4,1024,64]{1,2,0:T(8,128)(2,1)} %bitcast.76), calls=%async_computation.4 | async-start | bytes 1048576 | tf_op jit(solution)/shard_map/all_to_all | solution.py:17
  41.0 1.4 convolution_convert_fusion.1
  42.4 4.4 %copy.97 = bf16[64,128,256]{2,1,0:T(8,128)(2,1)} copy(bf16[64,128,256]{2,0,1:T(8,128)(2,1)S(1)} %convolution_convert_fusion.1) | data formatting | bytes 8388608 | tf_op jit(solution)/shard_map/convert_element_type | solution.py:65
  47.5 8.4 %all-to-all-start.3 = ((bf16[64,128,256]{2,1,0:T(8,128)(2,1)}), bf16[64,128,256]{2,1,0:T(8,128)(2,1)}, u32[]{:S(2)}, u32[]{:S(2)}) async-start(bf16[64,128,256]{2,1,0:T(8,128)(2,1)} %copy.97), calls=%async_computation.3 | async-start | bytes 8388608 | tf_op jit(solution)/shard_map/all_to_all | solution.py:68
  55.9 67.5 %while.25 = (s32[]{:T(128)}, bf16[8,8,128,256]{3,2,1,0:T(8,128)(2,1)}, bf16[8,8,128,1024]{3,2,1,0:T(8,128)(2,1)}, s32[8,8,128,4]{2,3,1,0:T(4,128)}, s32[8,8,128]...) while((s32[]{:T(128)}, bf16[8,8,128,256]{3,2,1,0:T(8,128)(2,1)}, ...), condition=%wide.region_2.3_spmd, body=%wide.region_0.2_spmd.sunk | while | flops 552865792 | bytes 9572453 | solution.py:51
  57.4 4.0 %fusion.59 = bf16[8,128,1024]{2,1,0:T(8,128)(2,1)S(1)} fusion(s32[8,128,4]{1,2,0:T(4,128)S(1)} %copy.142, pred[8,128,4]{1,2,0:T(4,128)(4,1)S(1)} %iota_compare_fusion.5), kind=kLoop, calls=%fused_computation.3.clone.1 | loop fusion | flops 15728640 | bytes 2117632 | tf_op jit(solution)/shard_map/while/body/eval_jaxpr/reduce_sum | solution.py:13
  61.4 1.6 fusion.60
  62.9 1.5 bitcast_dynamic-update-slice_fusion.2
  65.9 4.0 %fusion.59 = bf16[8,128,1024]{2,1,0:T(8,128)(2,1)S(1)} fusion(s32[8,128,4]{1,2,0:T(4,128)S(1)} %copy.142, pred[8,128,4]{1,2,0:T(4,128)(4,1)S(1)} %iota_compare_fusion.5), kind=kLoop, calls=%fused_computation.3.clone.1 | loop fusion | flops 15728640 | bytes 2117632 | tf_op jit(solution)/shard_map/while/body/eval_jaxpr/reduce_sum | solution.py:13
  69.8 1.6 fusion.60
  71.4 1.5 bitcast_dynamic-update-slice_fusion.2
  74.3 4.0 %fusion.59 = bf16[8,128,1024]{2,1,0:T(8,128)(2,1)S(1)} fusion(s32[8,128,4]{1,2,0:T(4,128)S(1)} %copy.142, pred[8,128,4]{1,2,0:T(4,128)(4,1)S(1)} %iota_compare_fusion.5), kind=kLoop, calls=%fused_computation.3.clone.1 | loop fusion | flops 15728640 | bytes 2117632 | tf_op jit(solution)/shard_map/while/body/eval_jaxpr/reduce_sum | solution.py:13
  78.3 1.5 fusion.60
  79.8 1.5 bitcast_dynamic-update-slice_fusion.2
  82.7 4.0 %fusion.59 = bf16[8,128,1024]{2,1,0:T(8,128)(2,1)S(1)} fusion(s32[8,128,4]{1,2,0:T(4,128)S(1)} %copy.142, pred[8,128,4]{1,2,0:T(4,128)(4,1)S(1)} %iota_compare_fusion.5), kind=kLoop, calls=%fused_computation.3.clone.1 | loop fusion | flops 15728640 | bytes 2117632 | tf_op jit(solution)/shard_map/while/body/eval_jaxpr/reduce_sum | solution.py:13
  86.7 1.5 fusion.60
  88.2 1.5 bitcast_dynamic-update-slice_fusion.2
  91.1 4.0 %fusion.59 = bf16[8,128,1024]{2,1,0:T(8,128)(2,1)S(1)} fusion(s32[8,128,4]{1,2,0:T(4,128)S(1)} %copy.142, pred[8,128,4]{1,2,0:T(4,128)(4,1)S(1)} %iota_compare_fusion.5), kind=kLoop, calls=%fused_computation.3.clone.1 | loop fusion | flops 15728640 | bytes 2117632 | tf_op jit(solution)/shard_map/while/body/eval_jaxpr/reduce_sum | solution.py:13
  95.1 1.5 fusion.60
  96.6 1.5 bitcast_dynamic-update-slice_fusion.2
  99.6 4.0 %fusion.59 = bf16[8,128,1024]{2,1,0:T(8,128)(2,1)S(1)} fusion(s32[8,128,4]{1,2,0:T(4,128)S(1)} %copy.142, pred[8,128,4]{1,2,0:T(4,128)(4,1)S(1)} %iota_compare_fusion.5), kind=kLoop, calls=%fused_computation.3.clone.1 | loop fusion | flops 15728640 | bytes 2117632 | tf_op jit(solution)/shard_map/while/body/eval_jaxpr/reduce_sum | solution.py:13
  103.6 1.5 fusion.60
  105.1 1.5 bitcast_dynamic-update-slice_fusion.2
  108.0 4.0 %fusion.59 = bf16[8,128,1024]{2,1,0:T(8,128)(2,1)S(1)} fusion(s32[8,128,4]{1,2,0:T(4,128)S(1)} %copy.142, pred[8,128,4]{1,2,0:T(4,128)(4,1)S(1)} %iota_compare_fusion.5), kind=kLoop, calls=%fused_computation.3.clone.1 | loop fusion | flops 15728640 | bytes 2117632 | tf_op jit(solution)/shard_map/while/body/eval_jaxpr/reduce_sum | solution.py:13
  112.0 1.5 fusion.60
  113.5 1.5 bitcast_dynamic-update-slice_fusion.2
  116.4 4.0 %fusion.59 = bf16[8,128,1024]{2,1,0:T(8,128)(2,1)S(1)} fusion(s32[8,128,4]{1,2,0:T(4,128)S(1)} %copy.142, pred[8,128,4]{1,2,0:T(4,128)(4,1)S(1)} %iota_compare_fusion.5), kind=kLoop, calls=%fused_computation.3.clone.1 | loop fusion | flops 15728640 | bytes 2117632 | tf_op jit(solution)/shard_map/while/body/eval_jaxpr/reduce_sum | solution.py:13
  120.4 1.5 fusion.60
  121.9 1.5 bitcast_dynamic-update-slice_fusion.2
  123.4 5.5 %fusion.22 = bf16[64,128,256]{2,0,1:T(8,128)(2,1)S(1)} fusion(bf16[64,128,256]{2,1,0:T(8,128)(2,1)} %bitcast.98, s32[64]{0:T(128)S(1)} %bitcast.106), kind=kOutput, calls=%fused_computation.28 | convolution fusion | flops 270536704 | bytes 8388864 | tf_op jit(solution)/shard_map/np,pbd->nbd/dot_general | solution.py:53
  128.9 4.4 %copy.93 = bf16[64,128,256]{2,1,0:T(8,128)(2,1)} copy(bf16[64,128,256]{2,0,1:T(8,128)(2,1)S(1)} %fusion.22) | data formatting | bytes 8388608 | tf_op jit(solution)/shard_map/convert_element_type | solution.py:55
  133.3 18.6 %all-to-all-done.3 = bf16[64,128,256]{2,1,0:T(8,128)(2,1)} async-done(((bf16[64,128,256]{2,1,0:T(8,128)(2,1)}), bf16[64,128,256]{2,1,0:T(8,128)(2,1)}, u32[]{:S(2)}, u32[]{:S(2)}) %all-to-all-start.3) | async-done | bytes 4194336 | tf_op jit(solution)/shard_map/all_to_all | solution.py:68
  151.9 6.0 %all-to-all-start.2 = ((bf16[64,128,256]{2,1,0:T(8,128)(2,1)}), bf16[64,128,256]{2,1,0:T(8,128)(2,1)}, u32[]{:S(2)}, u32[]{:S(2)}) async-start(bf16[64,128,256]{2,1,0:T(8,128)(2,1)} %copy.93), calls=%async_computation.2 | async-start | bytes 8388608 | tf_op jit(solution)/shard_map/all_to_all | solution.py:57
  157.9 7.4 %convert_bitcast_fusion = bf16[8,8,128,256]{3,1,0,2:T(8,128)(2,1)} fusion(bf16[64,128,256]{2,1,0:T(8,128)(2,1)} %all-to-all-done.3, s32[64]{0:T(128)S(1)} %bitcast.107), kind=kOutput, calls=%fused_computation.27 | convolution fusion | flops 270536704 | bytes 8388864 | tf_op jit(solution)/shard_map/np,nbd->pbd/dot_general | solution.py:69
  165.3 37.3 %while.26 = (s32[]{:T(128)}, f32[1024,256]{1,0:T(8,128)}, bf16[8,8,128,1024]{3,2,1,0:T(8,128)(2,1)}, bf16[8,8,128,256]{3,1,0,2:T(8,128)(2,1)}, s32[]{:T(128)}, /*index=5*/s32[]{:T(128)}) while((s32[]{:T(128)}, f32[1024,256]{1,0:T(8,128)}, bf16[8,8,128,1024]{3,2,1,0:T(8,128)(2,1)}, bf16[8,8,128,256]{3,1,0,2:T(8,128)(2,1)}, ...), condition=%wide.region_4.5_spmd.clone, body=%wide.region_3.4_spmd.clone.sunk | while | flops 537395200 | bytes 5767263 | solution.py:82
  165.3 1.1 constant_dynamic-slice_fusion.5
  166.4 3.3 %fusion.62 = f32[1024,256]{1,0:T(8,128)} fusion(bf16[8,8,128,1024]{3,2,1,0:T(8,128)(2,1)} %get-tuple-element.309, s32[]{:T(128)S(6)} %copy.157, f32[1024,256]{1,0:T(8,128)} %get-tuple-element.302, bf16[1,8,128,256]{3,1,0,2:T(8,128)(2,1)S(1)} %constant_dynamic-slice_fusion.5, pred[]{:T(512)S(6)} %compare.3), kind=kOutput, calls=%fused_computation.17.clone.1 | convolution fusion | flops 537395200 | bytes 4718597 | tf_op jit(solution)/shard_map/while/body/eval_jaxpr/gbr,gbd->rd/dot_general | solution.py:77
  169.7 1.1 constant_dynamic-slice_fusion.5
  170.8 3.6 %fusion.62 = f32[1024,256]{1,0:T(8,128)} fusion(bf16[8,8,128,1024]{3,2,1,0:T(8,128)(2,1)} %get-tuple-element.309, s32[]{:T(128)S(6)} %copy.157, f32[1024,256]{1,0:T(8,128)} %get-tuple-element.302, bf16[1,8,128,256]{3,1,0,2:T(8,128)(2,1)S(1)} %constant_dynamic-slice_fusion.5, pred[]{:T(512)S(6)} %compare.3), kind=kOutput, calls=%fused_computation.17.clone.1 | convolution fusion | flops 537395200 | bytes 4718597 | tf_op jit(solution)/shard_map/while/body/eval_jaxpr/gbr,gbd->rd/dot_general | solution.py:77
  174.4 1.1 constant_dynamic-slice_fusion.5
  175.5 3.6 %fusion.62 = f32[1024,256]{1,0:T(8,128)} fusion(bf16[8,8,128,1024]{3,2,1,0:T(8,128)(2,1)} %get-tuple-element.309, s32[]{:T(128)S(6)} %copy.157, f32[1024,256]{1,0:T(8,128)} %get-tuple-element.302, bf16[1,8,128,256]{3,1,0,2:T(8,128)(2,1)S(1)} %constant_dynamic-slice_fusion.5, pred[]{:T(512)S(6)} %compare.3), kind=kOutput, calls=%fused_computation.17.clone.1 | convolution fusion | flops 537395200 | bytes 4718597 | tf_op jit(solution)/shard_map/while/body/eval_jaxpr/gbr,gbd->rd/dot_general | solution.py:77
  179.1 1.1 constant_dynamic-slice_fusion.5
  180.2 3.6 %fusion.62 = f32[1024,256]{1,0:T(8,128)} fusion(bf16[8,8,128,1024]{3,2,1,0:T(8,128)(2,1)} %get-tuple-element.309, s32[]{:T(128)S(6)} %copy.157, f32[1024,256]{1,0:T(8,128)} %get-tuple-element.302, bf16[1,8,128,256]{3,1,0,2:T(8,128)(2,1)S(1)} %constant_dynamic-slice_fusion.5, pred[]{:T(512)S(6)} %compare.3), kind=kOutput, calls=%fused_computation.17.clone.1 | convolution fusion | flops 537395200 | bytes 4718597 | tf_op jit(solution)/shard_map/while/body/eval_jaxpr/gbr,gbd->rd/dot_general | solution.py:77
  183.8 1.1 constant_dynamic-slice_fusion.5
  184.9 3.6 %fusion.62 = f32[1024,256]{1,0:T(8,128)} fusion(bf16[8,8,128,1024]{3,2,1,0:T(8,128)(2,1)} %get-tuple-element.309, s32[]{:T(128)S(6)} %copy.157, f32[1024,256]{1,0:T(8,128)} %get-tuple-element.302, bf16[1,8,128,256]{3,1,0,2:T(8,128)(2,1)S(1)} %constant_dynamic-slice_fusion.5, pred[]{:T(512)S(6)} %compare.3), kind=kOutput, calls=%fused_computation.17.clone.1 | convolution fusion | flops 537395200 | bytes 4718597 | tf_op jit(solution)/shard_map/while/body/eval_jaxpr/gbr,gbd->rd/dot_general | solution.py:77
  188.5 1.1 constant_dynamic-slice_fusion.5
  189.6 3.6 %fusion.62 = f32[1024,256]{1,0:T(8,128)} fusion(bf16[8,8,128,1024]{3,2,1,0:T(8,128)(2,1)} %get-tuple-element.309, s32[]{:T(128)S(6)} %copy.157, f32[1024,256]{1,0:T(8,128)} %get-tuple-element.302, bf16[1,8,128,256]{3,1,0,2:T(8,128)(2,1)S(1)} %constant_dynamic-slice_fusion.5, pred[]{:T(512)S(6)} %compare.3), kind=kOutput, calls=%fused_computation.17.clone.1 | convolution fusion | flops 537395200 | bytes 4718597 | tf_op jit(solution)/shard_map/while/body/eval_jaxpr/gbr,gbd->rd/dot_general | solution.py:77
  193.2 1.1 constant_dynamic-slice_fusion.5
  194.2 3.6 %fusion.62 = f32[1024,256]{1,0:T(8,128)} fusion(bf16[8,8,128,1024]{3,2,1,0:T(8,128)(2,1)} %get-tuple-element.309, s32[]{:T(128)S(6)} %copy.157, f32[1024,256]{1,0:T(8,128)} %get-tuple-element.302, bf16[1,8,128,256]{3,1,0,2:T(8,128)(2,1)S(1)} %constant_dynamic-slice_fusion.5, pred[]{:T(512)S(6)} %compare.3), kind=kOutput, calls=%fused_computation.17.clone.1 | convolution fusion | flops 537395200 | bytes 4718597 | tf_op jit(solution)/shard_map/while/body/eval_jaxpr/gbr,gbd->rd/dot_general | solution.py:77
  197.8 1.1 constant_dynamic-slice_fusion.5
  198.9 3.6 %fusion.62 = f32[1024,256]{1,0:T(8,128)} fusion(bf16[8,8,128,1024]{3,2,1,0:T(8,128)(2,1)} %get-tuple-element.309, s32[]{:T(128)S(6)} %copy.157, f32[1024,256]{1,0:T(8,128)} %get-tuple-element.302, bf16[1,8,128,256]{3,1,0,2:T(8,128)(2,1)S(1)} %constant_dynamic-slice_fusion.5, pred[]{:T(512)S(6)} %compare.3), kind=kOutput, calls=%fused_computation.17.clone.1 | convolution fusion | flops 537395200 | bytes 4718597 | tf_op jit(solution)/shard_map/while/body/eval_jaxpr/gbr,gbd->rd/dot_general | solution.py:77
  202.5 2.5 copy.101
  205.1 2.6 bitcast_add_fusion
  207.7 2.0 copy.105
  209.7 1.3 copy.106
  211.0 42.7 %all-to-all-done.2 = bf16[64,128,256]{2,1,0:T(8,128)(2,1)} async-done(((bf16[64,128,256]{2,1,0:T(8,128)(2,1)}), bf16[64,128,256]{2,1,0:T(8,128)(2,1)}, u32[]{:S(2)}, u32[]{:S(2)}) %all-to-all-start.2) | async-done | bytes 4194336 | tf_op jit(solution)/shard_map/all_to_all | solution.py:57
  253.7 4.5 %fusion.27 = bf16[16,128,256]{2,0,1:T(8,128)(2,1)S(1)} fusion(bf16[64,128,256]{2,1,0:T(8,128)(2,1)} %all-to-all-done.2, f32[64]{0:T(128)S(1)} %convert_reduce_fusion, f32[16]{0:T(128)S(1)} %iota_add_fusion), kind=kOutput, calls=%fused_computation.30 | convolution fusion | flops 67634176 | bytes 5243200 | tf_op jit(solution)/shard_map/tn,nbd->tbd/dot_general | solution.py:66
  258.3 1.3 copy.95
  (54 shorter events, 15.3 us)
Async XLA Ops:
  0.6 40.4 %copy-start = (bf16[2048,256]{1,0:T(8,128)(2,1)S(1)}, bf16[2048,256]{1,0:T(8,128)(2,1)}, u32[]{:S(2)}) copy-start(bf16[2048,256]{1,0:T(8,128)(2,1)} %param.17) | copy-start | bytes 3145732
  2.3 22.4 %all-to-all-start = ((bf16[64,1,1]{2,1,0:T(2,128)(2,1)}), bf16[64,1,1]{2,1,0:T(2,128)(2,1)S(1)}, u32[]{:S(2)}, u32[]{:S(2)}) async-start(bf16[64,1,1]{2,1,0:T(2,128)(2,1)} %copy.86), calls=%async_computation | async-start | bytes 65536 | tf_op jit(solution)/shard_map/all_to_all | solution.py:58
  24.7 12.3 %all-to-all-start.1 = ((bf16[4,1024,64]{1,2,0:T(8,128)(2,1)}), bf16[4,1024,64]{1,2,0:T(8,128)(2,1)S(1)}, u32[]{:S(2)}, u32[]{:S(2)}) async-start(bf16[4,1024,64]{1,2,0:T(8,128)(2,1)} %bitcast.77), calls=%async_computation.1 | async-start | bytes 1048576 | tf_op jit(solution)/shard_map/all_to_all | solution.py:30
  37.0 10.5 %all-to-all-start.4 = ((bf16[4,1024,64]{1,2,0:T(8,128)(2,1)}), bf16[4,1024,64]{1,2,0:T(8,128)(2,1)S(1)}, u32[]{:S(2)}, u32[]{:S(2)}) async-start(bf16[4,1024,64]{1,2,0:T(8,128)(2,1)} %bitcast.76), calls=%async_computation.4 | async-start | bytes 1048576 | tf_op jit(solution)/shard_map/all_to_all | solution.py:17
  47.5 104.3 %all-to-all-start.3 = ((bf16[64,128,256]{2,1,0:T(8,128)(2,1)}), bf16[64,128,256]{2,1,0:T(8,128)(2,1)}, u32[]{:S(2)}, u32[]{:S(2)}) async-start(bf16[64,128,256]{2,1,0:T(8,128)(2,1)} %copy.97), calls=%async_computation.3 | async-start | bytes 8388608 | tf_op jit(solution)/shard_map/all_to_all | solution.py:68
  55.9 67.5 %copy-start.1 = (s32[1,64]{1,0:T(1,128)S(1)}, s32[1,64]{1,0:T(1,128)}, u32[]{:S(2)}) copy-start(s32[1,64]{1,0:T(1,128)} %param.15) | copy-start | bytes 772
  151.9 101.9 %all-to-all-start.2 = ((bf16[64,128,256]{2,1,0:T(8,128)(2,1)}), bf16[64,128,256]{2,1,0:T(8,128)(2,1)}, u32[]{:S(2)}, u32[]{:S(2)}) async-start(bf16[64,128,256]{2,1,0:T(8,128)(2,1)} %copy.93), calls=%async_computation.2 | async-start | bytes 8388608 | tf_op jit(solution)/shard_map/all_to_all | solution.py:57
where the time goes:
time: 261 us; the launch traced here: 260 us
  waiting for transfers between devices  75.3 us (29%)
  matrix products  60.5 us (23%)
  local copies, waits for them, and re-layouts  51.6 us (20%)
  other arithmetic  36.2 us (14%)
  starting transfers between devices  35.1 us (13%)
    all_to_all x1, waiting for transfers between devices, per_device(): lax.all_to_all(send_blocks, 'table', split_axis=0, concat_axis=0, tiled=T...  42.7 us
    reduce_sum x8, other arithmetic, incidence(): return jnp.sum(hits.astype(jnp.bfloat16), axis=2)  31.6 us
    dot_general x8, matrix products, add_group(): jnp.einsum('gbr,gbd->rd', counts, grads, preferred_element_type=jnp.float32)  28.6 us
    all_to_all x1, waiting for transfers between devices, per_device(): lax.all_to_all(back_blocks, 'table', split_axis=0, concat_axis=0, tiled=T...  18.6 us
    all_to_all x1, starting transfers between devices, per_device(): lax.all_to_all(send_tiles, 'table', split_axis=0, concat_axis=0, tiled=True)  13.2 us
    dot_general x8, matrix products, pool_group(): jnp.einsum('gbr,rd->gbd', counts, owned, preferred_element_type=jnp.float32)  12.2 us
    dynamic_update_slice x8, local copies, waits for them, and re-layouts, per_device(): lax.map(pool_group, (rows_grouped, lens_grouped))  12 us
    dynamic_slice x8, local copies, waits for them, and re-layouts, per_device(): grad, unused = lax.scan(add_group, empty, (saved_counts, pair_grads))  8.6 us
  transfers between devices with their start and end apart: 5, of which 5 were waited for; matrix products, arithmetic and copies ran while one was open for 54% of the time, Pallas kernels for 0%

commit v1 on v0

--- a/solution.py
+++ b/solution.py
@@ -27,7 +27,10 @@
     tile_count = pooled_grad.shape[0] // bag_rows
     span = min(8, pair_count)
     groups = pair_count // span
-    owned = lax.all_to_all(embedding, "col", split_axis=0, concat_axis=1, tiled=True)
+    owned = jnp.concatenate(
+        lax.all_to_all(jnp.stack(jnp.split(embedding, lax.axis_size("col"), axis=0)), "col", 0, 0),
+        axis=1,
+    )
     state = move_state(accumulator)
     row_count = owned.shape[0]
     rows_grouped = pair_rows.reshape(groups, span, bag_rows, pair_rows.shape[2])

time: 261 us -> 261 us (level)
  no operation moved by 1% of the time
where the time goes in v1:
time: 261 us; the launch traced here: 260 us
  waiting for transfers between devices  75.8 us (29%)
  matrix products  60.6 us (23%)
  local copies, waits for them, and re-layouts  51.1 us (20%)
  other arithmetic  36.2 us (14%)
  starting transfers between devices  35.1 us (13%)
    all_to_all x1, waiting for transfers between devices, per_device(): lax.all_to_all(send_blocks, 'table', split_axis=0, concat_axis=0, tiled=T...  43.3 us
    reduce_sum x8, other arithmetic, incidence(): return jnp.sum(hits.astype(jnp.bfloat16), axis=2)  31.6 us
    dot_general x8, matrix products, add_group(): jnp.einsum('gbr,gbd->rd', counts, grads, preferred_element_type=jnp.float32)  28.6 us
    all_to_all x1, waiting for transfers between devices, per_device(): lax.all_to_all(back_blocks, 'table', split_axis=0, concat_axis=0, tiled=T...  18.5 us
    all_to_all x1, starting transfers between devices, per_device(): lax.all_to_all(send_tiles, 'table', split_axis=0, concat_axis=0, tiled=True)  13.2 us
    dot_general x8, matrix products, pool_group(): jnp.einsum('gbr,rd->gbd', counts, owned, preferred_element_type=jnp.float32)  12.3 us
    dynamic_update_slice x8, local copies, waits for them, and re-layouts, per_device(): lax.map(pool_group, (rows_grouped, lens_grouped))  12 us
    dynamic_slice x8, local copies, waits for them, and re-layouts, per_device(): grad, unused = lax.scan(add_group, empty, (saved_counts, pair_grads))  8.6 us
  transfers between devices with their start and end apart: 5, of which 5 were waited for; matrix products, arithmetic and copies ran while one was open for 54% of the time, Pallas kernels for 0%

profile of v1, /device:TPU:1, one launch (start us, length us, event | category | flops | bytes accessed | tf_op | source)
XLA Modules:
  0.0 259.6 jit_solution(669951487323519894)
XLA Ops:
  2.3 13.2 %all-to-all-start = ((bf16[64,1,1]{2,1,0:T(2,128)(2,1)}), bf16[64,1,1]{2,1,0:T(2,128)(2,1)S(1)}, u32[]{:S(2)}, u32[]{:S(2)}) async-start(bf16[64,1,1]{2,1,0:T(2,128)(2,1)} %copy.83), calls=%async_computation | async-start | bytes 65536 | tf_op jit(solution)/shard_map/all_to_all | solution.py:61
  15.5 1.1 slice_bitcast_fusion.3
  17.5 7.2 %all-to-all-done = bf16[64,1,1]{2,1,0:T(2,128)(2,1)S(1)} async-done(((bf16[64,1,1]{2,1,0:T(2,128)(2,1)}), bf16[64,1,1]{2,1,0:T(2,128)(2,1)S(1)}, u32[]{:S(2)}, u32[]{:S(2)}) %all-to-all-start) | async-done | bytes 160 | tf_op jit(solution)/shard_map/all_to_all | solution.py:61
  24.7 4.0 %all-to-all-start.1 = ((bf16[4,1024,64]{1,2,0:T(8,128)(2,1)}), bf16[4,1024,64]{1,2,0:T(8,128)(2,1)S(1)}, u32[]{:S(2)}, u32[]{:S(2)}) async-start(bf16[4,1024,64]{1,2,0:T(8,128)(2,1)} %pad_maximum_fusion), calls=%async_computation.1 | async-start | bytes 1048576 | tf_op jit(solution)/shard_map/all_to_all | solution.py:31
  28.7 1.3 convert_element_type.78
  30.9 6.2 %all-to-all-done.1 = bf16[4,1024,64]{1,2,0:T(8,128)(2,1)S(1)} async-done(((bf16[4,1024,64]{1,2,0:T(8,128)(2,1)}), bf16[4,1024,64]{1,2,0:T(8,128)(2,1)S(1)}, u32[]{:S(2)}, u32[]{:S(2)}) %all-to-all-start.1) | async-done | bytes 524320 | tf_op jit(solution)/shard_map/all_to_all | solution.py:31
  37.0 3.5 %all-to-all-start.4 = ((bf16[4,1024,64]{1,2,0:T(8,128)(2,1)}), bf16[4,1024,64]{1,2,0:T(8,128)(2,1)S(1)}, u32[]{:S(2)}, u32[]{:S(2)}) async-start(bf16[4,1024,64]{1,2,0:T(8,128)(2,1)} %bitcast.81), calls=%async_computation.4 | async-start | bytes 1048576 | tf_op jit(solution)/shard_map/all_to_all | solution.py:17
  41.0 1.4 convolution_convert_fusion.1
  42.4 4.4 %copy.93 = bf16[64,128,256]{2,1,0:T(8,128)(2,1)} copy(bf16[64,128,256]{2,0,1:T(8,128)(2,1)S(1)} %convolution_convert_fusion.1) | data formatting | bytes 8388608 | tf_op jit(solution)/shard_map/convert_element_type | solution.py:68
  47.5 8.4 %all-to-all-start.3 = ((bf16[64,128,256]{2,1,0:T(8,128)(2,1)}), bf16[64,128,256]{2,1,0:T(8,128)(2,1)}, u32[]{:S(2)}, u32[]{:S(2)}) async-start(bf16[64,128,256]{2,1,0:T(8,128)(2,1)} %copy.93), calls=%async_computation.3 | async-start | bytes 8388608 | tf_op jit(solution)/shard_map/all_to_all | solution.py:71
  55.9 67.5 %while.25 = (s32[]{:T(128)}, bf16[8,8,128,256]{3,2,1,0:T(8,128)(2,1)}, bf16[8,8,128,1024]{3,2,1,0:T(8,128)(2,1)}, s32[8,8,128,4]{2,3,1,0:T(4,128)}, s32[8,8,128]...) while((s32[]{:T(128)}, bf16[8,8,128,256]{3,2,1,0:T(8,128)(2,1)}, ...), condition=%wide.region_2.3_spmd, body=%wide.region_0.2_spmd.sunk | while | flops 552865792 | bytes 9573461 | solution.py:54
  57.4 4.0 %fusion.59 = bf16[8,128,1024]{2,1,0:T(8,128)(2,1)S(1)} fusion(s32[8,128,4]{1,2,0:T(4,128)S(1)} %copy.135, pred[8,128,4]{1,2,0:T(4,128)(4,1)S(1)} %iota_compare_fusion.5), kind=kLoop, calls=%fused_computation.3.clone.1 | loop fusion | flops 15728640 | bytes 2117632 | tf_op jit(solution)/shard_map/while/body/eval_jaxpr/reduce_sum | solution.py:13
  61.4 1.6 fusion.60
  62.9 1.5 bitcast_dynamic-update-slice_fusion.2
  65.8 4.0 %fusion.59 = bf16[8,128,1024]{2,1,0:T(8,128)(2,1)S(1)} fusion(s32[8,128,4]{1,2,0:T(4,128)S(1)} %copy.135, pred[8,128,4]{1,2,0:T(4,128)(4,1)S(1)} %iota_compare_fusion.5), kind=kLoop, calls=%fused_computation.3.clone.1 | loop fusion | flops 15728640 | bytes 2117632 | tf_op jit(solution)/shard_map/while/body/eval_jaxpr/reduce_sum | solution.py:13
  69.8 1.6 fusion.60
  71.4 1.5 bitcast_dynamic-update-slice_fusion.2
  74.3 4.0 %fusion.59 = bf16[8,128,1024]{2,1,0:T(8,128)(2,1)S(1)} fusion(s32[8,128,4]{1,2,0:T(4,128)S(1)} %copy.135, pred[8,128,4]{1,2,0:T(4,128)(4,1)S(1)} %iota_compare_fusion.5), kind=kLoop, calls=%fused_computation.3.clone.1 | loop fusion | flops 15728640 | bytes 2117632 | tf_op jit(solution)/shard_map/while/body/eval_jaxpr/reduce_sum | solution.py:13
  78.3 1.5 fusion.60
  79.8 1.5 bitcast_dynamic-update-slice_fusion.2
  82.7 4.0 %fusion.59 = bf16[8,128,1024]{2,1,0:T(8,128)(2,1)S(1)} fusion(s32[8,128,4]{1,2,0:T(4,128)S(1)} %copy.135, pred[8,128,4]{1,2,0:T(4,128)(4,1)S(1)} %iota_compare_fusion.5), kind=kLoop, calls=%fused_computation.3.clone.1 | loop fusion | flops 15728640 | bytes 2117632 | tf_op jit(solution)/shard_map/while/body/eval_jaxpr/reduce_sum | solution.py:13
  86.7 1.5 fusion.60
  88.2 1.5 bitcast_dynamic-update-slice_fusion.2
  91.2 4.0 %fusion.59 = bf16[8,128,1024]{2,1,0:T(8,128)(2,1)S(1)} fusion(s32[8,128,4]{1,2,0:T(4,128)S(1)} %copy.135, pred[8,128,4]{1,2,0:T(4,128)(4,1)S(1)} %iota_compare_fusion.5), kind=kLoop, calls=%fused_computation.3.clone.1 | loop fusion | flops 15728640 | bytes 2117632 | tf_op jit(solution)/shard_map/while/body/eval_jaxpr/reduce_sum | solution.py:13
  95.1 1.5 fusion.60
  96.7 1.5 bitcast_dynamic-update-slice_fusion.2
  99.6 4.0 %fusion.59 = bf16[8,128,1024]{2,1,0:T(8,128)(2,1)S(1)} fusion(s32[8,128,4]{1,2,0:T(4,128)S(1)} %copy.135, pred[8,128,4]{1,2,0:T(4,128)(4,1)S(1)} %iota_compare_fusion.5), kind=kLoop, calls=%fused_computation.3.clone.1 | loop fusion | flops 15728640 | bytes 2117632 | tf_op jit(solution)/shard_map/while/body/eval_jaxpr/reduce_sum | solution.py:13
  103.6 1.5 fusion.60
  105.1 1.5 bitcast_dynamic-update-slice_fusion.2
  108.1 4.0 %fusion.59 = bf16[8,128,1024]{2,1,0:T(8,128)(2,1)S(1)} fusion(s32[8,128,4]{1,2,0:T(4,128)S(1)} %copy.135, pred[8,128,4]{1,2,0:T(4,128)(4,1)S(1)} %iota_compare_fusion.5), kind=kLoop, calls=%fused_computation.3.clone.1 | loop fusion | flops 15728640 | bytes 2117632 | tf_op jit(solution)/shard_map/while/body/eval_jaxpr/reduce_sum | solution.py:13
  112.0 1.5 fusion.60
  113.5 1.5 bitcast_dynamic-update-slice_fusion.2
  116.5 4.0 %fusion.59 = bf16[8,128,1024]{2,1,0:T(8,128)(2,1)S(1)} fusion(s32[8,128,4]{1,2,0:T(4,128)S(1)} %copy.135, pred[8,128,4]{1,2,0:T(4,128)(4,1)S(1)} %iota_compare_fusion.5), kind=kLoop, calls=%fused_computation.3.clone.1 | loop fusion | flops 15728640 | bytes 2117632 | tf_op jit(solution)/shard_map/while/body/eval_jaxpr/reduce_sum | solution.py:13
  120.4 1.5 fusion.60
  122.0 1.5 bitcast_dynamic-update-slice_fusion.2
  123.4 5.5 %fusion.22 = bf16[64,128,256]{2,0,1:T(8,128)(2,1)S(1)} fusion(bf16[64,128,256]{2,1,0:T(8,128)(2,1)} %bitcast.102, s32[64]{0:T(128)S(1)} %bitcast.109), kind=kOutput, calls=%fused_computation.28 | convolution fusion | flops 270536704 | bytes 8388864 | tf_op jit(solution)/shard_map/np,pbd->nbd/dot_general | solution.py:56
  128.9 4.4 %copy.89 = bf16[64,128,256]{2,1,0:T(8,128)(2,1)} copy(bf16[64,128,256]{2,0,1:T(8,128)(2,1)S(1)} %fusion.22) | data formatting | bytes 8388608 | tf_op jit(solution)/shard_map/convert_element_type | solution.py:58
  133.3 18.5 %all-to-all-done.3 = bf16[64,128,256]{2,1,0:T(8,128)(2,1)} async-done(((bf16[64,128,256]{2,1,0:T(8,128)(2,1)}), bf16[64,128,256]{2,1,0:T(8,128)(2,1)}, u32[]{:S(2)}, u32[]{:S(2)}) %all-to-all-start.3) | async-done | bytes 4194336 | tf_op jit(solution)/shard_map/all_to_all | solution.py:71
  151.8 6.0 %all-to-all-start.2 = ((bf16[64,128,256]{2,1,0:T(8,128)(2,1)}), bf16[64,128,256]{2,1,0:T(8,128)(2,1)}, u32[]{:S(2)}, u32[]{:S(2)}) async-start(bf16[64,128,256]{2,1,0:T(8,128)(2,1)} %copy.89), calls=%async_computation.2 | async-start | bytes 8388608 | tf_op jit(solution)/shard_map/all_to_all | solution.py:60
  157.9 7.4 %convert_bitcast_fusion = bf16[8,8,128,256]{3,1,0,2:T(8,128)(2,1)} fusion(bf16[64,128,256]{2,1,0:T(8,128)(2,1)} %all-to-all-done.3, s32[64]{0:T(128)S(1)} %bitcast.110), kind=kOutput, calls=%fused_computation.27 | convolution fusion | flops 270536704 | bytes 8388864 | tf_op jit(solution)/shard_map/np,nbd->pbd/dot_general | solution.py:72
  165.3 37.3 %while.26 = (s32[]{:T(128)}, f32[1024,256]{1,0:T(8,128)}, bf16[8,8,128,1024]{3,2,1,0:T(8,128)(2,1)}, bf16[8,8,128,256]{3,1,0,2:T(8,128)(2,1)}, s32[]{:T(128)}, /*index=5*/s32[]{:T(128)}) while((s32[]{:T(128)}, f32[1024,256]{1,0:T(8,128)}, bf16[8,8,128,1024]{3,2,1,0:T(8,128)(2,1)}, bf16[8,8,128,256]{3,1,0,2:T(8,128)(2,1)}, ...), condition=%wide.region_4.5_spmd.clone, body=%wide.region_3.4_spmd.clone.sunk | while | flops 537395200 | bytes 5767763 | solution.py:85
  165.3 1.1 constant_dynamic-slice_fusion.5
  166.4 3.3 %fusion.62 = f32[1024,256]{1,0:T(8,128)} fusion(bf16[8,8,128,1024]{3,2,1,0:T(8,128)(2,1)} %get-tuple-element.313, s32[]{:T(128)} %get-tuple-element.305, f32[1024,256]{1,0:T(8,128)} %get-tuple-element.306, bf16[1,8,128,256]{3,1,0,2:T(8,128)(2,1)S(1)} %constant_dynamic-slice_fusion.5, pred[]{:T(512)S(6)} %compare.3), kind=kOutput, calls=%fused_computation.17.clone.1 | convolution fusion | flops 537395200 | bytes 4719105 | tf_op jit(solution)/shard_map/while/body/eval_jaxpr/gbr,gbd->rd/dot_general | solution.py:80
  169.7 1.1 constant_dynamic-slice_fusion.5
  170.8 3.6 %fusion.62 = f32[1024,256]{1,0:T(8,128)} fusion(bf16[8,8,128,1024]{3,2,1,0:T(8,128)(2,1)} %get-tuple-element.313, s32[]{:T(128)} %get-tuple-element.305, f32[1024,256]{1,0:T(8,128)} %get-tuple-element.306, bf16[1,8,128,256]{3,1,0,2:T(8,128)(2,1)S(1)} %constant_dynamic-slice_fusion.5, pred[]{:T(512)S(6)} %compare.3), kind=kOutput, calls=%fused_computation.17.clone.1 | convolution fusion | flops 537395200 | bytes 4719105 | tf_op jit(solution)/shard_map/while/body/eval_jaxpr/gbr,gbd->rd/dot_general | solution.py:80
  174.4 1.1 constant_dynamic-slice_fusion.5
  175.5 3.6 %fusion.62 = f32[1024,256]{1,0:T(8,128)} fusion(bf16[8,8,128,1024]{3,2,1,0:T(8,128)(2,1)} %get-tuple-element.313, s32[]{:T(128)} %get-tuple-element.305, f32[1024,256]{1,0:T(8,128)} %get-tuple-element.306, bf16[1,8,128,256]{3,1,0,2:T(8,128)(2,1)S(1)} %constant_dynamic-slice_fusion.5, pred[]{:T(512)S(6)} %compare.3), kind=kOutput, calls=%fused_computation.17.clone.1 | convolution fusion | flops 537395200 | bytes 4719105 | tf_op jit(solution)/shard_map/while/body/eval_jaxpr/gbr,gbd->rd/dot_general | solution.py:80
  179.1 1.1 constant_dynamic-slice_fusion.5
  180.2 3.6 %fusion.62 = f32[1024,256]{1,0:T(8,128)} fusion(bf16[8,8,128,1024]{3,2,1,0:T(8,128)(2,1)} %get-tuple-element.313, s32[]{:T(128)} %get-tuple-element.305, f32[1024,256]{1,0:T(8,128)} %get-tuple-element.306, bf16[1,8,128,256]{3,1,0,2:T(8,128)(2,1)S(1)} %constant_dynamic-slice_fusion.5, pred[]{:T(512)S(6)} %compare.3), kind=kOutput, calls=%fused_computation.17.clone.1 | convolution fusion | flops 537395200 | bytes 4719105 | tf_op jit(solution)/shard_map/while/body/eval_jaxpr/gbr,gbd->rd/dot_general | solution.py:80
  183.8 1.1 constant_dynamic-slice_fusion.5
  184.9 3.6 %fusion.62 = f32[1024,256]{1,0:T(8,128)} fusion(bf16[8,8,128,1024]{3,2,1,0:T(8,128)(2,1)} %get-tuple-element.313, s32[]{:T(128)} %get-tuple-element.305, f32[1024,256]{1,0:T(8,128)} %get-tuple-element.306, bf16[1,8,128,256]{3,1,0,2:T(8,128)(2,1)S(1)} %constant_dynamic-slice_fusion.5, pred[]{:T(512)S(6)} %compare.3), kind=kOutput, calls=%fused_computation.17.clone.1 | convolution fusion | flops 537395200 | bytes 4719105 | tf_op jit(solution)/shard_map/while/body/eval_jaxpr/gbr,gbd->rd/dot_general | solution.py:80
  188.5 1.1 constant_dynamic-slice_fusion.5
  189.6 3.6 %fusion.62 = f32[1024,256]{1,0:T(8,128)} fusion(bf16[8,8,128,1024]{3,2,1,0:T(8,128)(2,1)} %get-tuple-element.313, s32[]{:T(128)} %get-tuple-element.305, f32[1024,256]{1,0:T(8,128)} %get-tuple-element.306, bf16[1,8,128,256]{3,1,0,2:T(8,128)(2,1)S(1)} %constant_dynamic-slice_fusion.5, pred[]{:T(512)S(6)} %compare.3), kind=kOutput, calls=%fused_computation.17.clone.1 | convolution fusion | flops 537395200 | bytes 4719105 | tf_op jit(solution)/shard_map/while/body/eval_jaxpr/gbr,gbd->rd/dot_general | solution.py:80
  193.2 1.1 constant_dynamic-slice_fusion.5
  194.2 3.6 %fusion.62 = f32[1024,256]{1,0:T(8,128)} fusion(bf16[8,8,128,1024]{3,2,1,0:T(8,128)(2,1)} %get-tuple-element.313, s32[]{:T(128)} %get-tuple-element.305, f32[1024,256]{1,0:T(8,128)} %get-tuple-element.306, bf16[1,8,128,256]{3,1,0,2:T(8,128)(2,1)S(1)} %constant_dynamic-slice_fusion.5, pred[]{:T(512)S(6)} %compare.3), kind=kOutput, calls=%fused_computation.17.clone.1 | convolution fusion | flops 537395200 | bytes 4719105 | tf_op jit(solution)/shard_map/while/body/eval_jaxpr/gbr,gbd->rd/dot_general | solution.py:80
  197.8 1.1 constant_dynamic-slice_fusion.5
  198.9 3.6 %fusion.62 = f32[1024,256]{1,0:T(8,128)} fusion(bf16[8,8,128,1024]{3,2,1,0:T(8,128)(2,1)} %get-tuple-element.313, s32[]{:T(128)} %get-tuple-element.305, f32[1024,256]{1,0:T(8,128)} %get-tuple-element.306, bf16[1,8,128,256]{3,1,0,2:T(8,128)(2,1)S(1)} %constant_dynamic-slice_fusion.5, pred[]{:T(512)S(6)} %compare.3), kind=kOutput, calls=%fused_computation.17.clone.1 | convolution fusion | flops 537395200 | bytes 4719105 | tf_op jit(solution)/shard_map/while/body/eval_jaxpr/gbr,gbd->rd/dot_general | solution.py:80
  202.5 1.6 copy.97
  204.1 1.7 bitcast_add_fusion
  205.8 2.5 copy.102
  208.4 2.0 copy.101
  210.4 43.3 %all-to-all-done.2 = bf16[64,128,256]{2,1,0:T(8,128)(2,1)} async-done(((bf16[64,128,256]{2,1,0:T(8,128)(2,1)}), bf16[64,128,256]{2,1,0:T(8,128)(2,1)}, u32[]{:S(2)}, u32[]{:S(2)}) %all-to-all-start.2) | async-done | bytes 4194336 | tf_op jit(solution)/shard_map/all_to_all | solution.py:60
  253.7 4.5 %fusion.27 = bf16[16,128,256]{2,0,1:T(8,128)(2,1)S(1)} fusion(bf16[64,128,256]{2,1,0:T(8,128)(2,1)} %all-to-all-done.2, f32[64]{0:T(128)S(1)} %convert_reduce_fusion, f32[16]{0:T(128)S(1)} %iota_add_fusion), kind=kOutput, calls=%fused_computation.30 | convolution fusion | flops 67634176 | bytes 5243200 | tf_op jit(solution)/shard_map/tn,nbd->tbd/dot_general | solution.py:69
  258.3 1.3 copy.91
  (55 shorter events, 16.1 us)
Async XLA Ops:
  0.6 40.4 %copy-start = (bf16[2048,256]{1,0:T(8,128)(2,1)S(1)}, bf16[2048,256]{1,0:T(8,128)(2,1)}, u32[]{:S(2)}) copy-start(bf16[2048,256]{1,0:T(8,128)(2,1)} %param.17) | copy-start | bytes 3145732
  2.3 22.4 %all-to-all-start = ((bf16[64,1,1]{2,1,0:T(2,128)(2,1)}), bf16[64,1,1]{2,1,0:T(2,128)(2,1)S(1)}, u32[]{:S(2)}, u32[]{:S(2)}) async-start(bf16[64,1,1]{2,1,0:T(2,128)(2,1)} %copy.83), calls=%async_computation | async-start | bytes 65536 | tf_op jit(solution)/shard_map/all_to_all | solution.py:61
  24.7 12.3 %all-to-all-start.1 = ((bf16[4,1024,64]{1,2,0:T(8,128)(2,1)}), bf16[4,1024,64]{1,2,0:T(8,128)(2,1)S(1)}, u32[]{:S(2)}, u32[]{:S(2)}) async-start(bf16[4,1024,64]{1,2,0:T(8,128)(2,1)} %pad_maximum_fusion), calls=%async_computation.1 | async-start | bytes 1048576 | tf_op jit(solution)/shard_map/all_to_all | solution.py:31
  37.0 10.5 %all-to-all-start.4 = ((bf16[4,1024,64]{1,2,0:T(8,128)(2,1)}), bf16[4,1024,64]{1,2,0:T(8,128)(2,1)S(1)}, u32[]{:S(2)}, u32[]{:S(2)}) async-start(bf16[4,1024,64]{1,2,0:T(8,128)(2,1)} %bitcast.81), calls=%async_computation.4 | async-start | bytes 1048576 | tf_op jit(solution)/shard_map/all_to_all | solution.py:17
  47.5 104.3 %all-to-all-start.3 = ((bf16[64,128,256]{2,1,0:T(8,128)(2,1)}), bf16[64,128,256]{2,1,0:T(8,128)(2,1)}, u32[]{:S(2)}, u32[]{:S(2)}) async-start(bf16[64,128,256]{2,1,0:T(8,128)(2,1)} %copy.93), calls=%async_computation.3 | async-start | bytes 8388608 | tf_op jit(solution)/shard_map/all_to_all | solution.py:71
  55.9 67.5 %copy-start.1 = (s32[1,64]{1,0:T(1,128)S(1)}, s32[1,64]{1,0:T(1,128)}, u32[]{:S(2)}) copy-start(s32[1,64]{1,0:T(1,128)} %param.15) | copy-start | bytes 772
  151.8 101.9 %all-to-all-start.2 = ((bf16[64,128,256]{2,1,0:T(8,128)(2,1)}), bf16[64,128,256]{2,1,0:T(8,128)(2,1)}, u32[]{:S(2)}, u32[]{:S(2)}) async-start(bf16[64,128,256]{2,1,0:T(8,128)(2,1)} %copy.89), calls=%async_computation.2 | async-start | bytes 8388608 | tf_op jit(solution)/shard_map/all_to_all | solution.py:60
